TPU v7x, 128 devices: a whole 4x4x4 slice. The times are simulated.
128 devices in a mesh: group: 4 (over x), gy: 4 (over z_lo, core), gx: 8 (over z_hi, y).
Axes of the slice: x: 4, y: 4, z: 4 (z_hi: 2, z_lo: 2; z = z_hi * 2 + z_lo), core: 2. Of those that a mesh axis runs over, the one named last changes fastest.
Arguments:
- east_velocity: float32 [24, 64, 4, 1024], P('group', 'gy', None, 'gx'), may hold values from -6 to 6
- north_velocity: float32 [24, 64, 4, 1024], P('group', 'gy', None, 'gx'), may hold values from -6 to 6
- sea_surface: float32 [64, 4, 1024], P('gy', None, 'gx'), may hold values from -6 to 6
- tracers: float32 [30, 24, 64, 4096], P(None, None, 'gy', ('group', 'gx')), may hold values from -6 to 6
- land_sea: int32 [64, 4096], P('gy', ('group', 'gx')), may hold values 0 or 1
- bottom_level: int32 [64, 4096], P('gy', ('group', 'gx')), may hold values from 1 to 24
- coupling: float32 [30, 30], replicated, may hold values from -1 to 1
Outputs:
- tracers_next: float32 [30, 24, 64, 4096], P(None, None, 'gy', ('group', 'gx'))
- surface_next: float32 [64, 4, 1024], P('gy', None, 'gx')
All inputs are finite; a program needn't handle non-finite values. No bound on the sum of `land_sea` on one device may be relied on, other than what follows from the above.
Results may differ from a plain program's by a relative error of at most 0.0003.
Values sent between devices are 32-bit elements; how exact they have to be, the bound alone decides.
A program may use at most 128 MiB of HBM per device.

v0:
```python
import functools

import jax
import jax.numpy as jnp
from jax import lax
from jax.experimental import pallas as pl
from jax.experimental.pallas import tpu as pltpu
from jax.sharding import PartitionSpec as P

CORIOLIS = 0.5
GRAVITY = 0.3
VISCOSITY = 0.1
TIME_STEP = 0.2
BAROTROPIC = 0.5
ADVECTION = 0.15
MIXING = 0.5
KAPPA_BASE = 0.1
KAPPA_SHEAR = 2.0
SHEAR_SCALE = 1.0
ECOLOGY = 0.2

MESH = pl.DeviceIdType.MESH
ANY = pl.BlockSpec(memory_space=pl.ANY)

T = 30
Z = 24
G = 4
L = Z // G
Y = 16
X = 128
PLANES = 2 * L + 1
FOLDED = Y * G
TILE_ROWS = 2 * L * Y
EDGE_ROWS = T * Z + 8
EDGE_COLS = Z * 8 + 8
CHUNKS = 3


def roll(x, by, axis):
    by = by % x.shape[axis]
    return x if by == 0 else pltpu.roll(x, by, axis)


def lanes(shape):
    return lax.broadcasted_iota(jnp.int32, shape, len(shape) - 1)


def rows(shape):
    return lax.broadcasted_iota(jnp.int32, shape, 0)


def exchange_kernel(
    n_gy,
    n_gx,
    u_hbm,
    v_hbm,
    eta_hbm,
    c_hbm,
    land_hbm,
    bottom_hbm,
    coupling_hbm,
    tiles,
    south_rows,
    north_rows,
    west_cols,
    east_cols,
    west_u,
    south_v,
    mix_hi_out,
    mix_lo_out,
    planes,
    conc,
    land,
    bottom,
    coupling,
    edge_q,
    west_q,
    east_q,
    fresh,
    col_pack,
    send_tile,
    send_u,
    send_v,
    row_lo,
    row_hi,
    col_q,
    mix_hi,
    mix_lo,
    load_sem,
    conc_sem,
    send_sem,
    recv_sem,
    tile_send,
    tile_recv,
    u_send,
    u_recv,
    v_send,
    v_recv,
    store_sem,
):
    g = lax.axis_index("group")
    j = lax.axis_index("gy")
    i = lax.axis_index("gx")
    i_east = lax.rem(i + 1, n_gx)
    i_west = lax.rem(i + n_gx - 1, n_gx)
    has_south = j > 0
    has_north = j < n_gy - 1

    loads = [
        pltpu.make_async_copy(u_hbm, planes.at[pl.ds(0, L), pl.ds(8, FOLDED)], load_sem.at[0]),
        pltpu.make_async_copy(v_hbm, planes.at[pl.ds(L, L), pl.ds(8, FOLDED)], load_sem.at[1]),
        pltpu.make_async_copy(eta_hbm, planes.at[2 * L, pl.ds(8, FOLDED)], load_sem.at[2]),
        pltpu.make_async_copy(land_hbm, land, load_sem.at[3]),
        pltpu.make_async_copy(bottom_hbm, bottom, load_sem.at[4]),
        pltpu.make_async_copy(coupling_hbm, coupling, load_sem.at[5]),
    ]
    for load in loads:
        load.start()
    part_rows = T * Z * Y // CHUNKS
    conc_loads = [
        pltpu.make_async_copy(
            c_hbm.at[pl.ds(n * part_rows, part_rows)],
            conc.at[pl.ds(n * part_rows, part_rows)],
            conc_sem.at[n],
        )
        for n in range(CHUNKS)
    ]
    for load in conc_loads:
        load.start()

    barrier = pltpu.get_barrier_semaphore()
    for d in range(1, G):
        pl.semaphore_signal(barrier, inc=1, device_id=(lax.rem(g + d, G), j, i), device_id_type=MESH)
    for d in range(G):
        pl.semaphore_signal(barrier, inc=1, device_id=(d, j, i_east), device_id_type=MESH)
        pl.semaphore_signal(barrier, inc=1, device_id=(d, j, i_west), device_id_type=MESH)

    @pl.when(has_south)
    def _():
        for d in range(G):
            pl.semaphore_signal(barrier, inc=1, device_id=(d, j - 1, i), device_id_type=MESH)

    @pl.when(has_north)
    def _():
        for d in range(G):
            pl.semaphore_signal(barrier, inc=1, device_id=(d, j + 1, i), device_id_type=MESH)

    for load in loads:
        load.wait()
    lane = lanes((FOLDED, X))
    packed = jnp.zeros((FOLDED, X), jnp.float32)
    for p in range(PLANES):
        packed = jnp.where(lane // 2 == p, roll(planes[p, 8 : 8 + FOLDED, :], 2 * p + 1, 1), packed)
    edge_q[...] = packed

    around = lax.div(j + n_gy - 1, n_gy) + lax.div(2 * (n_gy - 1) - j, n_gy)
    pl.semaphore_wait(barrier, G - 1 + 2 * G + G * around)

    def remote(src, dst, n, device):
        return pltpu.make_async_remote_copy(
            src_ref=src,
            dst_ref=dst,
            send_sem=send_sem.at[n],
            recv_sem=recv_sem.at[n],
            device_id=device,
            device_id_type=MESH,
        )

    to_north = remote(planes.at[:, pl.ds(FOLDED, 8)], planes.at[:, pl.ds(0, 8)], 0, (g, j + 1, i))
    to_south = remote(
        planes.at[:, pl.ds(8, 8)], planes.at[:, pl.ds(8 + FOLDED, 8)], 1, (g, j - 1, i)
    )
    to_east = remote(edge_q, west_q, 2, (g, j, i_east))
    to_west = remote(edge_q, east_q, 3, (g, j, i_west))
    to_east.start()
    to_west.start()

    @pl.when(has_north)
    def _():
        to_north.start()

    @pl.when(has_south)
    def _():
        to_south.start()

    depth = jnp.where(land[...] > 0, bottom[...], 0).astype(jnp.float32)
    row_lo[pl.ds(T * Z, 8), :] = jnp.broadcast_to(depth[0:1], (8, X))
    row_hi[pl.ds(T * Z, 8), :] = jnp.broadcast_to(depth[Y - 1 : Y], (8, X))
    for n in range(CHUNKS):
        conc_loads[n].wait()

        def take_rows(t, carry):
            base = pl.multiple_of(t * (Z * Y), Z * Y)
            place = pl.multiple_of(t * Z, 8)
            row_lo[pl.ds(place, Z), :] = conc[pl.ds(base, Z, stride=Y), :]
            row_hi[pl.ds(place, Z), :] = conc[pl.ds(base + Y - 1, Z, stride=Y), :]
            return carry

        lax.fori_loop(n * (T // CHUNKS), (n + 1) * (T // CHUNKS), take_rows, 0)

    rows_north = remote(row_hi, south_rows, 4, (g, j + 1, i))
    rows_south = remote(row_lo, north_rows, 5, (g, j - 1, i))

    @pl.when(has_north)
    def _():
        rows_north.start()

    @pl.when(has_south)
    def _():
        rows_south.start()

    @pl.when(has_south)
    def _():
        to_north.wait_recv()

    @pl.when(has_north)
    def _():
        to_south.wait_recv()

    @pl.when(jnp.logical_not(has_south))
    def _():
        planes[:, pl.ds(0, 8), :] = jnp.zeros((PLANES, 8, X), jnp.float32)

    @pl.when(jnp.logical_not(has_north))
    def _():
        planes[:, pl.ds(8 + FOLDED, 8), :] = jnp.zeros((PLANES, 8, X), jnp.float32)

    to_east.wait_recv()
    to_west.wait_recv()
    fold = lax.rem(rows((FOLDED, X)), G)
    qw = west_q[...]
    qe = east_q[...]
    qw_turned = jnp.where(fold == 0, roll(qw, -(G - 1), 0), roll(qw, 1, 0))
    qe_turned = jnp.where(fold == G - 1, roll(qe, G - 1, 0), roll(qe, -1, 0))
    qw = jnp.where(i == 0, qw_turned, qw)
    qe = jnp.where(i == n_gx - 1, qe_turned, qe)
    west_q[...] = jnp.where(lane % 2 == 1, roll(qw, 1, 1), roll(qe, -1, 1))

    def eastern(x, edge):
        return jnp.where(lane == X - 1, edge, roll(x, -1, 1))

    def western(x, edge):
        return jnp.where(lane == 0, edge, roll(x, 1, 1))

    def sides(p):
        return roll(west_q[...], -(2 * p + 1), 1)

    def at(p, shift):
        return planes[p, 8 + shift : 8 + shift + FOLDED, :]

    height = at(2 * L, 0)
    push_east = GRAVITY * (eastern(height, sides(2 * L)) - height)
    push_north = GRAVITY * (at(2 * L, G) - height)
    spread = jnp.zeros((FOLDED, X), jnp.float32)
    pack = jnp.zeros((FOLDED, X), jnp.float32)
    for k in range(L):
        u = at(k, 0)
        v = at(L + k, 0)
        u_side = sides(k)
        v_side = sides(L + k)
        u_west = western(u, u_side)
        v_south = at(L + k, -G)
        lap_u = eastern(u, u_side) + u_west + at(k, G) + at(k, -G) - 4.0 * u
        lap_v = eastern(v, v_side) + western(v, v_side) + at(L + k, G) + v_south - 4.0 * v
        u_new = u + TIME_STEP * (CORIOLIS * v - push_east + VISCOSITY * lap_u)
        v_new = v + TIME_STEP * (-CORIOLIS * u - push_north + VISCOSITY * lap_v)
        spread = spread + (u - u_west + v - v_south)
        fresh[pl.ds(k * FOLDED, FOLDED), :] = u_new
        fresh[pl.ds((L + k) * FOLDED, FOLDED), :] = v_new
        pack = jnp.where(lane == k, roll(u_new, k + 1, 1), pack)
    col_pack[...] = pack
    for f in range(G):
        for p in range(2 * L):
            send_tile[f, pl.ds(p * Y, Y), :] = fresh[pl.ds(p * FOLDED + f, Y, stride=G), :]
        send_tile[f, pl.ds(TILE_ROWS, FOLDED), :] = spread
        send_u[f] = col_pack[pl.ds(f, Y, stride=G), :]
        send_v[f] = jnp.zeros((8, X), jnp.float32)
        send_v[f, pl.ds(0, L), :] = fresh[
            pl.ds(L * FOLDED + (Y - 1) * G + f, L, stride=FOLDED), :
        ]

    def tile_copy(d):
        other = lax.rem(g + d, G)
        return pltpu.make_async_remote_copy(
            src_ref=send_tile.at[other],
            dst_ref=tiles.at[g],
            send_sem=tile_send.at[other],
            recv_sem=tile_recv.at[g],
            device_id=(other, j, i),
            device_id_type=MESH,
        )

    def u_copy(f):
        crossed = jnp.where(i == n_gx - 1, 1, 0)
        return pltpu.make_async_remote_copy(
            src_ref=send_u.at[f],
            dst_ref=west_u.at[g],
            send_sem=u_send.at[f],
            recv_sem=u_recv.at[g],
            device_id=(lax.rem(f + crossed, G), j, i_east),
            device_id_type=MESH,
        )

    def v_copy(f):
        return pltpu.make_async_remote_copy(
            src_ref=send_v.at[f],
            dst_ref=south_v.at[g],
            send_sem=v_send.at[f],
            recv_sem=v_recv.at[g],
            device_id=(f, j + 1, i),
            device_id_type=MESH,
        )

    for d in (2, 1, 3):
        tile_copy(d).start()
    for f in range(G):
        u_copy(f).start()

    @pl.when(has_north)
    def _():
        for f in range(G):
            v_copy(f).start()

    own_tile = pltpu.make_async_copy(send_tile.at[g], tiles.at[g], store_sem.at[0])
    own_tile.start()

    small = lanes((8, X))

    def take_cols(z, carry):
        parts = [jnp.zeros((8, X), jnp.float32) for _ in range(4)]
        for t in range(T):
            for o in range(2):
                base = pl.multiple_of(t * (Z * Y) + z * Y + 8 * o, 8)
                n = (2 * t + o) % 4
                parts[n] = jnp.where(
                    small // 2 == 32 * o + t,
                    roll(conc[pl.ds(base, 8), :], 64 * o + 2 * t + 1, 1),
                    parts[n],
                )
        col_q[pl.ds(pl.multiple_of(z * 8, 8), 8), :] = (parts[0] + parts[1]) + (
            parts[2] + parts[3]
        )
        return carry

    lax.fori_loop(0, Z, take_cols, 0)
    col_q[pl.ds(Z * 8, 8), :] = jnp.where(
        small // 2 == 0,
        roll(depth[0:8], 1, 1),
        jnp.where(small // 2 == 32, roll(depth[8:16], 65, 1), 0.0),
    )
    up = jnp.where(i == n_gx - 1, 1, 0)
    down = jnp.where(i == 0, G - 1, 0)
    cols_east = remote(col_q, west_cols, 6, (lax.rem(g + up, G), j, i_east))
    cols_west = remote(col_q, east_cols, 7, (lax.rem(g + down, G), j, i_west))
    cols_east.start()
    cols_west.start()

    tall = (rows((8 * T, T)) // 8 == lanes((8 * T, T))).astype(jnp.bfloat16)
    wide = (rows((T, 8 * T)) == lanes((T, 8 * T)) // 8).astype(jnp.bfloat16)
    own = lax.rem(rows((8 * T, 8 * T)), 8) == lax.rem(lanes((8 * T, 8 * T)), 8)
    hi = coupling[...].astype(jnp.bfloat16)
    lo = (coupling[...] - hi.astype(jnp.float32)).astype(jnp.bfloat16)
    for part, place in ((hi, mix_hi), (lo, mix_lo)):
        half = jnp.dot(tall, part, preferred_element_type=jnp.float32).astype(jnp.bfloat16)
        whole = jnp.dot(half, wide, preferred_element_type=jnp.float32)
        place[...] = jnp.where(own, whole, 0.0).astype(jnp.bfloat16)
    stores = [
        pltpu.make_async_copy(mix_hi, mix_hi_out, store_sem.at[1]),
        pltpu.make_async_copy(mix_lo, mix_lo_out, store_sem.at[2]),
    ]
    for store in stores:
        store.start()

    for d in range(1, G):
        other = lax.rem(g + d, G)
        pltpu.make_async_remote_copy(
            src_ref=send_tile.at[other],
            dst_ref=tiles.at[other],
            send_sem=tile_send.at[other],
            recv_sem=tile_recv.at[other],
            device_id=(other, j, i),
            device_id_type=MESH,
        ).wait()
    for f in range(G):
        pltpu.make_async_remote_copy(
            src_ref=send_u.at[f],
            dst_ref=west_u.at[f],
            send_sem=u_send.at[f],
            recv_sem=u_recv.at[f],
            device_id=(f, j, i_east),
            device_id_type=MESH,
        ).wait()

    @pl.when(has_north)
    def _():
        to_north.wait_send()
        rows_north.wait_send()
        rows_south.wait_recv()
        for f in range(G):
            v_copy(f).wait_send()

    @pl.when(has_south)
    def _():
        to_south.wait_send()
        rows_south.wait_send()
        rows_north.wait_recv()
        for f in range(G):
            pltpu.make_async_remote_copy(
                src_ref=send_v.at[f],
                dst_ref=south_v.at[f],
                send_sem=v_send.at[f],
                recv_sem=v_recv.at[f],
                device_id=(f, j - 1, i),
                device_id_type=MESH,
            ).wait_recv()

    to_east.wait_send()
    to_west.wait_send()
    cols_east.wait()
    cols_west.wait()
    own_tile.wait()
    for store in stores:
        store.wait()


def exchange(n_gy, n_gx, u, v, eta, conc, land, bottom, coupling):
    f32 = jnp.float32
    dma = pltpu.SemaphoreType.DMA
    out_shape = (
        jax.ShapeDtypeStruct((G, TILE_ROWS + FOLDED, X), f32),
        jax.ShapeDtypeStruct((EDGE_ROWS, X), f32),
        jax.ShapeDtypeStruct((EDGE_ROWS, X), f32),
        jax.ShapeDtypeStruct((EDGE_COLS, X), f32),
        jax.ShapeDtypeStruct((EDGE_COLS, X), f32),
        jax.ShapeDtypeStruct((G, Y, X), f32),
        jax.ShapeDtypeStruct((G, 8, X), f32),
        jax.ShapeDtypeStruct((8 * T, 8 * T), jnp.bfloat16),
        jax.ShapeDtypeStruct((8 * T, 8 * T), jnp.bfloat16),
    )
    return pl.pallas_call(
        functools.partial(exchange_kernel, n_gy, n_gx),
        out_shape=out_shape,
        in_specs=[ANY] * 7,
        out_specs=(ANY,) * 9,
        scratch_shapes=[
            pltpu.VMEM((PLANES, FOLDED + 16, X), f32),
            pltpu.VMEM((T * Z * Y, X), f32),
            pltpu.VMEM((Y, X), jnp.int32),
            pltpu.VMEM((Y, X), jnp.int32),
            pltpu.VMEM((T, T), f32),
            pltpu.VMEM((FOLDED, X), f32),
            pltpu.VMEM((FOLDED, X), f32),
            pltpu.VMEM((FOLDED, X), f32),
            pltpu.VMEM((2 * L * FOLDED, X), f32),
            pltpu.VMEM((FOLDED, X), f32),
            pltpu.VMEM((G, TILE_ROWS + FOLDED, X), f32),
            pltpu.VMEM((G, Y, X), f32),
            pltpu.VMEM((G, 8, X), f32),
            pltpu.VMEM((EDGE_ROWS, X), f32),
            pltpu.VMEM((EDGE_ROWS, X), f32),
            pltpu.VMEM((EDGE_COLS, X), f32),
            pltpu.VMEM((8 * T, 8 * T), jnp.bfloat16),
            pltpu.VMEM((8 * T, 8 * T), jnp.bfloat16),
            dma((6,)),
            dma((CHUNKS,)),
            dma((8,)),
            dma((8,)),
            dma((G,)),
            dma((G,)),
            dma((G,)),
            dma((G,)),
            dma((G,)),
            dma((G,)),
            dma((3,)),
        ],
        compiler_params=pltpu.CompilerParams(
            collective_id=0, has_side_effects=True, vmem_limit_bytes=32 * 1024 * 1024
        ),
        name="exchange",
    )(u, v, eta, conc, land, bottom, coupling)


Z_PART = 4
T_PART = 5
COEF = 9


def column_kernel(
    n_gy,
    c_hbm,
    tiles_hbm,
    south_rows_hbm,
    north_rows_hbm,
    west_cols_hbm,
    east_cols_hbm,
    west_u_hbm,
    south_v_hbm,
    mix_hi_hbm,
    mix_lo_hbm,
    eta_hbm,
    land_hbm,
    bottom_hbm,
    out_hbm,
    surface_hbm,
    conc,
    solved,
    coef,
    tiles,
    south_rows,
    north_rows,
    west_cols,
    east_cols,
    west_u,
    south_v,
    mix_hi,
    mix_lo,
    eta,
    land,
    bottom,
    surface,
    adv_a,
    adv_b,
    hi_a,
    lo_a,
    hi_b,
    lo_b,
    load_sem,
    conc_sem,
    out_sem,
):
    j = lax.axis_index("gy")
    pairs = (
        (land_hbm, land),
        (bottom_hbm, bottom),
        (tiles_hbm, tiles),
        (west_u_hbm, west_u),
        (south_v_hbm, south_v),
        (west_cols_hbm, west_cols),
        (east_cols_hbm, east_cols),
        (south_rows_hbm, south_rows),
        (north_rows_hbm, north_rows),
        (eta_hbm, eta),
        (mix_hi_hbm, mix_hi),
        (mix_lo_hbm, mix_lo),
    )
    loads = [pltpu.make_async_copy(a, b, load_sem.at[n]) for n, (a, b) in enumerate(pairs)]
    for load in loads:
        load.start()
    conc_loads = [
        pltpu.make_async_copy(
            c_hbm.at[:, pl.ds(n * Z_PART, Z_PART)],
            conc.at[:, pl.ds(n * Z_PART, Z_PART), pl.ds(8, Y)],
            conc_sem.at[n],
        )
        for n in range(Z // Z_PART)
    ]
    for load in conc_loads:
        load.start()
    for load in loads:
        load.wait()

    flat = conc.reshape(T * Z * 32, X)
    south_ok = j > 0
    north_ok = j < n_gy - 1

    def put_rows(t, carry):
        place = pl.multiple_of(t * Z, 8)
        base = pl.multiple_of(t * (Z * 32), 8)
        flat[pl.ds(base + 7, Z, stride=32), :] = jnp.where(
            south_ok, south_rows[pl.ds(place, Z), :], 0.0
        )
        flat[pl.ds(base + 8 + Y, Z, stride=32), :] = jnp.where(
            north_ok, north_rows[pl.ds(place, Z), :], 0.0
        )
        return carry

    lax.fori_loop(0, T, put_rows, 0)

    lane = lanes((8, X))
    odd = lane % 2 == 1

    def put_cols(z, carry):
        place = pl.ds(pl.multiple_of(z * 8, 8), 8)
        west_cols[place, :] = jnp.where(
            odd, roll(west_cols[place, :], 1, 1), roll(east_cols[place, :], -1, 1)
        )
        return carry

    lax.fori_loop(0, Z + 1, put_cols, 0)

    total = tiles[0, pl.ds(TILE_ROWS, FOLDED), :]
    for m in range(1, G):
        total = total + tiles[m, pl.ds(TILE_ROWS, FOLDED), :]
    surface[...] = eta[...] - (BAROTROPIC / Z) * total
    surface_store = pltpu.make_async_copy(surface, surface_hbm, out_sem.at[T // T_PART])
    surface_store.start()

    wide = lanes((Y, X))
    tall = rows((Y, X))
    depth = jnp.where(land[...] > 0, bottom[...], 0).astype(jnp.float32)
    depth_side = west_cols[pl.ds(Z * 8, 8), :]
    depth_side = jnp.concatenate([roll(depth_side, -1, 1), roll(depth_side, -65, 1)], axis=0)
    depth_east = jnp.where(wide == X - 1, depth_side, roll(depth, -1, 1))
    depth_west = jnp.where(wide == 0, depth_side, roll(depth, 1, 1))
    above = jnp.where(north_ok, north_rows[pl.ds(T * Z, 8), :], 0.0)
    below = jnp.where(south_ok, south_rows[pl.ds(T * Z, 8), :], 0.0)
    depth_north = jnp.where(
        tall == Y - 1, jnp.concatenate([above, above], axis=0), roll(depth, -1, 0)
    )
    depth_south = jnp.where(tall == 0, jnp.concatenate([below, below], axis=0), roll(depth, 1, 0))
    reach_east = jnp.minimum(depth, depth_east)
    reach_west = jnp.minimum(depth, depth_west)
    reach_north = jnp.minimum(depth, depth_north)
    reach_south = jnp.minimum(depth, depth_south)

    def flows(z):
        m, k = z // L, z % L
        return tiles[m, pl.ds(k * Y, Y), :], tiles[m, pl.ds((L + k) * Y, Y), :]

    g_above = jnp.zeros((Y, X), jnp.float32)
    r_above = jnp.zeros((Y, X), jnp.float32)
    u, v = flows(0)
    for z in range(Z):
        m, k = z // L, z % L
        u_west = jnp.where(wide == 0, roll(west_u[m], -k, 1), roll(u, 1, 1))
        row = jnp.where(south_ok, south_v[m, k : k + 1, :], 0.0)
        v_south = jnp.where(tall == 0, jnp.broadcast_to(row, (Y, X)), roll(v, 1, 0))
        ke = jnp.where(reach_east > z, ADVECTION, 0.0)
        kw = jnp.where(reach_west > z, ADVECTION, 0.0)
        kn = jnp.where(reach_north > z, ADVECTION, 0.0)
        ks = jnp.where(reach_south > z, ADVECTION, 0.0)
        coef[z, 0] = (
            1.0
            - ke * jnp.maximum(u, 0.0)
            + kw * jnp.minimum(u_west, 0.0)
            - kn * jnp.maximum(v, 0.0)
            + ks * jnp.minimum(v_south, 0.0)
        )
        coef[z, 1] = -ke * jnp.minimum(u, 0.0)
        coef[z, 2] = kw * jnp.maximum(u_west, 0.0)
        coef[z, 3] = -kn * jnp.minimum(v, 0.0)
        coef[z, 4] = ks * jnp.maximum(v_south, 0.0)
        if z < Z - 1:
            u_next, v_next = flows(z + 1)
            shear = (u - u_next) ** 2 + (v - v_next) ** 2
            rate = KAPPA_BASE + KAPPA_SHEAR * shear / (shear + SHEAR_SCALE)
            g = jnp.where(depth > z + 1, MIXING * rate, 0.0)
            u, v = u_next, v_next
        else:
            g = jnp.zeros((Y, X), jnp.float32)
        inverse = 1.0 / (1.0 + g_above + g - g_above * r_above)
        coef[z, 5] = inverse
        coef[z, 6] = jnp.where(depth > z, ECOLOGY * inverse, 0.0)
        coef[z, 7] = g_above * inverse
        r_above = g * inverse
        coef[z, 8] = r_above
        g_above = g

    def zero_top(t, carry):
        solved[t, 0] = jnp.zeros((Y, X), jnp.float32)
        return carry

    lax.fori_loop(0, T, zero_top, 0)

    def advance(z, adv, hi_ref, lo_ref):
        side = west_cols[pl.ds(pl.multiple_of(z * 8, 8), 8), :]
        for o in range(2):
            ks = [coef[z, n, 8 * o : 8 * o + 8, :] for n in range(5)]
            for pair in range(T // 2):
                both = []
                for t in (2 * pair, 2 * pair + 1):
                    c = conc[t, z, 8 + 8 * o : 16 + 8 * o, :]
                    edge = roll(side, -(64 * o + 2 * t + 1), 1)
                    east = jnp.where(lane == X - 1, edge, roll(c, -1, 1))
                    west = jnp.where(lane == 0, edge, roll(c, 1, 1))
                    north = conc[t, z, 9 + 8 * o : 17 + 8 * o, :]
                    south = conc[t, z, 7 + 8 * o : 15 + 8 * o, :]
                    a = (ks[0] * c + ks[1] * east) + (
                        ks[2] * west + (ks[3] * north + ks[4] * south)
                    )
                    adv[t, 8 * o : 8 * o + 8, :] = a
                    both.append(jnp.tanh(a))
                y = jnp.concatenate(both, axis=0)
                hi = y.astype(jnp.bfloat16)
                lo = (y - hi.astype(jnp.float32)).astype(jnp.bfloat16)
                hi_ref[16 * pair : 16 * pair + 16, o * X : o * X + X] = hi
                lo_ref[16 * pair : 16 * pair + 16, o * X : o * X + X] = lo

    def mix(hi_ref, lo_ref):
        return (
            jnp.dot(mix_hi[...], hi_ref[...], preferred_element_type=jnp.float32)
            + jnp.dot(mix_lo[...], hi_ref[...], preferred_element_type=jnp.float32)
            + jnp.dot(mix_hi[...], lo_ref[...], preferred_element_type=jnp.float32)
        )

    def finish(z, adv, source):
        for o in range(2):
            ks = [coef[z, n, 8 * o : 8 * o + 8, :] for n in range(5, 8)]
            for t in range(T):
                s = source[8 * t : 8 * t + 8, o * X : o * X + X]
                solved[t, z + 1, 8 * o : 8 * o + 8, :] = (
                    ks[0] * adv[t, 8 * o : 8 * o + 8, :]
                    + ks[1] * s
                    + ks[2] * solved[t, z, 8 * o : 8 * o + 8, :]
                )

    def two(i, carry):
        z = 2 * i

        source = mix(hi_a, lo_a)
        advance(z + 1, adv_b, hi_b, lo_b)
        finish(z, adv_a, source)
        source = mix(hi_b, lo_b)
        advance(z + 2, adv_a, hi_a, lo_a)
        finish(z + 1, adv_b, source)
        return carry

    for load in conc_loads:
        load.wait()
    advance(0, adv_a, hi_a, lo_a)
    lax.fori_loop(0, Z // 2 - 1, two, 0)
    source = mix(hi_a, lo_a)
    advance(Z - 1, adv_b, hi_b, lo_b)
    finish(Z - 2, adv_a, source)
    finish(Z - 1, adv_b, mix(hi_b, lo_b))

    def store(n):
        return pltpu.make_async_copy(
            solved.at[pl.ds(n * T_PART, T_PART), pl.ds(1, Z)],
            out_hbm.at[pl.ds(n * T_PART, T_PART)],
            out_sem.at[n],
        )

    def back(n, carry):
        base = n * T_PART
        x = [solved[base + t, Z] for t in range(T_PART)]
        for z in range(Z - 2, -1, -1):
            r = coef[z, 8]
            for t in range(T_PART):
                x[t] = solved[base + t, z + 1] + r * x[t]
                solved[base + t, z + 1] = x[t]
        store(n).start()
        return carry

    lax.fori_loop(0, T // T_PART, back, 0)
    for n in range(T // T_PART):
        store(n).wait()
    surface_store.wait()


def columns(n_gy, conc, parts, eta, land, bottom):
    f32 = jnp.float32
    dma = pltpu.SemaphoreType.DMA
    mix_type = pltpu.VMEM((8 * T, 2 * X), jnp.bfloat16)
    return pl.pallas_call(
        functools.partial(column_kernel, n_gy),
        out_shape=(
            jax.ShapeDtypeStruct((T, Z, Y, X), f32),
            jax.ShapeDtypeStruct((FOLDED, X), f32),
        ),
        in_specs=[ANY] * 13,
        out_specs=(ANY, ANY),
        scratch_shapes=[
            pltpu.VMEM((T, Z, 32, X), f32),
            pltpu.VMEM((T, Z + 1, Y, X), f32),
            pltpu.VMEM((Z, COEF, Y, X), f32),
            pltpu.VMEM((G, TILE_ROWS + FOLDED, X), f32),
            pltpu.VMEM((EDGE_ROWS, X), f32),
            pltpu.VMEM((EDGE_ROWS, X), f32),
            pltpu.VMEM((EDGE_COLS, X), f32),
            pltpu.VMEM((EDGE_COLS, X), f32),
            pltpu.VMEM((G, Y, X), f32),
            pltpu.VMEM((G, 8, X), f32),
            pltpu.VMEM((8 * T, 8 * T), jnp.bfloat16),
            pltpu.VMEM((8 * T, 8 * T), jnp.bfloat16),
            pltpu.VMEM((FOLDED, X), f32),
            pltpu.VMEM((Y, X), jnp.int32),
            pltpu.VMEM((Y, X), jnp.int32),
            pltpu.VMEM((FOLDED, X), f32),
            pltpu.VMEM((T, Y, X), f32),
            pltpu.VMEM((T, Y, X), f32),
            mix_type,
            mix_type,
            mix_type,
            mix_type,
            dma((12,)),
            dma((Z // Z_PART,)),
            dma((T // T_PART + 1,)),
        ],
        compiler_params=pltpu.CompilerParams(vmem_limit_bytes=48 * 1024 * 1024),
        name="columns",
    )(conc, *parts, eta, land, bottom)


def shards(east_velocity, north_velocity, sea_surface, tracers, land_sea, bottom_level, coupling):
    n_gy = lax.axis_size("gy")
    n_gx = lax.axis_size("gx")
    eta = sea_surface.reshape(FOLDED, X)
    parts = exchange(
        n_gy,
        n_gx,
        east_velocity.reshape(L, FOLDED, X),
        north_velocity.reshape(L, FOLDED, X),
        eta,
        tracers.reshape(T * Z * Y, X),
        land_sea,
        bottom_level,
        coupling,
    )
    tracers_next, surface_next = columns(n_gy, tracers, parts, eta, land_sea, bottom_level)
    return tracers_next, surface_next.reshape(Y, G, X)


def solution(mesh):
    placed = (
        P("group", "gy", None, "gx"),
        P("group", "gy", None, "gx"),
        P("gy", None, "gx"),
        P(None, None, "gy", ("group", "gx")),
        P("gy", ("group", "gx")),
        P("gy", ("group", "gx")),
        P(),
    )
    return jax.shard_map(
        shards,
        mesh=mesh,
        in_specs=placed,
        out_specs=(P(None, None, "gy", ("group", "gx")), P("gy", None, "gx")),
        check_vma=False,
    )
```

profile of v0, /device:TPU:1, one launch (start us, length us, event | category | flops | bytes accessed | tf_op | source)
XLA Modules:
  0.0 50.4 jit_solution(2494605275429179948)
XLA Ops:
  0.6 0.0 copy-start
  0.6 2.7 %copy-done = f32[30,24,16,128]{3,2,1,0:T(8,128)S(1)} copy-done((f32[30,24,16,128]{3,2,1,0:T(8,128)S(1)}, f32[30,24,16,128]{3,2,1,0:T(8,128)}, u32[]{:S(2)}) %copy-start) | copy-done | bytes 5898264
  3.3 0.0 copy-start.1
  3.3 0.9 %copy-done.1 = f32[6,16,4,128]{3,2,1,0:T(4,128)S(1)} copy-done((f32[6,16,4,128]{3,2,1,0:T(4,128)S(1)}, f32[6,16,4,128]{3,2,1,0:T(4,128)}, u32[]{:S(2)}) %copy-start.1) | copy-done | bytes 196632
  4.2 0.0 copy-start.2
  4.2 0.9 %copy-done.2 = f32[6,16,4,128]{3,2,1,0:T(4,128)S(1)} copy-done((f32[6,16,4,128]{3,2,1,0:T(4,128)S(1)}, f32[6,16,4,128]{3,2,1,0:T(4,128)}, u32[]{:S(2)}) %copy-start.2) | copy-done | bytes 196632
  5.2 0.0 copy-start.3
  5.2 0.8 %copy-done.3 = f32[16,4,128]{2,1,0:T(4,128)S(1)} copy-done((f32[16,4,128]{2,1,0:T(4,128)S(1)}, f32[16,4,128]{2,1,0:T(4,128)}, u32[]{:S(2)}) %copy-start.3) | copy-done | bytes 32792
  5.9 0.0 copy-start.5
  5.9 0.7 %copy-done.5 = s32[16,128]{1,0:T(8,128)S(1)} copy-done((s32[16,128]{1,0:T(8,128)S(1)}, s32[16,128]{1,0:T(8,128)}, u32[]{:S(2)}) %copy-start.5) | copy-done | bytes 8216
  6.6 0.0 copy-start.7
  6.6 0.7 %copy-done.7 = s32[16,128]{1,0:T(8,128)S(1)} copy-done((s32[16,128]{1,0:T(8,128)S(1)}, s32[16,128]{1,0:T(8,128)}, u32[]{:S(2)}) %copy-start.7) | copy-done | bytes 8216
  7.3 0.0 copy-start.9
  7.3 0.7 %copy-done.9 = f32[30,30]{1,0:T(8,128)S(1)} copy-done((f32[30,30]{1,0:T(8,128)S(1)}, f32[30,30]{1,0:T(8,128)}, u32[]{:S(2)}) %copy-start.9) | copy-done | bytes 3624
  8.0 0.0 copy-start.4
  8.0 0.0 copy-start.6
  8.0 0.0 copy-start.8
  8.0 27.5 %exchange.1 = (f32[4,256,128]{2,1,0:T(8,128)S(1)}, f32[728,128]{1,0:T(8,128)S(1)}, f32[728,128]{1,0:T(8,128)S(1)}, f32[200,128]{1,0:T(8,128)S(1)}, f32[200,128]{...) custom-call(f32[6,64,128]{2,1,0:T(8,128)S(1)} %bitcast.6, ...), custom_call_target="tpu_custom_call" | custom-call | tf_op jit(solution)/shard_map/exchange/pallas_call | solution.py:440
  35.6 0.0 copy-done.4
  35.6 0.0 copy-done.6
  35.6 0.0 copy-done.8
  35.6 14.8 %columns.1 = (f32[30,24,16,128]{3,2,1,0:T(8,128)}, f32[64,128]{1,0:T(8,128)}) custom-call(f32[30,24,16,128]{3,2,1,0:T(8,128)} %c_hbm.1, f32[4,256,128]{2,1,0:T(8,128)S(1)} %get-tuple-element.13.tiles_hbm, f32[728,128]{1,0:T(8,128)S(1)} %get-tuple-element.14.south_rows_hbm, f32[728,128]{1,0:T(8,128)S(1)} %get-tuple-element.15.north_rows_hbm, ...), custom_call_target="tpu_custom_call" | custom-call | tf_op jit(solution)/shard_map/columns/pallas_call | solution.py:755
Async XLA Ops:
  0.6 2.7 %copy-start = (f32[30,24,16,128]{3,2,1,0:T(8,128)S(1)}, f32[30,24,16,128]{3,2,1,0:T(8,128)}, u32[]{:S(2)}) copy-start(f32[30,24,16,128]{3,2,1,0:T(8,128)} %c_hbm.1) | copy-start | bytes 17694724
  3.3 0.9 %copy-start.1 = (f32[6,16,4,128]{3,2,1,0:T(4,128)S(1)}, f32[6,16,4,128]{3,2,1,0:T(4,128)}, u32[]{:S(2)}) copy-start(f32[6,16,4,128]{3,2,1,0:T(4,128)} %param.7) | copy-start | bytes 589828
  4.2 0.9 %copy-start.2 = (f32[6,16,4,128]{3,2,1,0:T(4,128)S(1)}, f32[6,16,4,128]{3,2,1,0:T(4,128)}, u32[]{:S(2)}) copy-start(f32[6,16,4,128]{3,2,1,0:T(4,128)} %param.8) | copy-start | bytes 589828
  5.2 0.8 %copy-start.3 = (f32[16,4,128]{2,1,0:T(4,128)S(1)}, f32[16,4,128]{2,1,0:T(4,128)}, u32[]{:S(2)}) copy-start(f32[16,4,128]{2,1,0:T(4,128)} %param.9) | copy-start | bytes 98308
  5.9 0.7 %copy-start.5 = (s32[16,128]{1,0:T(8,128)S(1)}, s32[16,128]{1,0:T(8,128)}, u32[]{:S(2)}) copy-start(s32[16,128]{1,0:T(8,128)} %land_hbm.3) | copy-start | bytes 24580
  6.6 0.7 %copy-start.7 = (s32[16,128]{1,0:T(8,128)S(1)}, s32[16,128]{1,0:T(8,128)}, u32[]{:S(2)}) copy-start(s32[16,128]{1,0:T(8,128)} %bottom_hbm.3) | copy-start | bytes 24580
  7.3 0.7 %copy-start.9 = (f32[30,30]{1,0:T(8,128)S(1)}, f32[30,30]{1,0:T(8,128)}, u32[]{:S(2)}) copy-start(f32[30,30]{1,0:T(8,128)} %coupling_hbm.1) | copy-start | bytes 10804
  8.0 27.5 %copy-start.4 = (f32[16,4,128]{2,1,0:T(4,128)S(1)}, f32[16,4,128]{2,1,0:T(4,128)}, u32[]{:S(2)}) copy-start(f32[16,4,128]{2,1,0:T(4,128)} %param.9) | copy-start | bytes 98308
  8.0 27.6 %copy-start.6 = (s32[16,128]{1,0:T(8,128)S(1)}, s32[16,128]{1,0:T(8,128)}, u32[]{:S(2)}) copy-start(s32[16,128]{1,0:T(8,128)} %land_hbm.3) | copy-start | bytes 24580
  8.0 27.6 %copy-start.8 = (s32[16,128]{1,0:T(8,128)S(1)}, s32[16,128]{1,0:T(8,128)}, u32[]{:S(2)}) copy-start(s32[16,128]{1,0:T(8,128)} %bottom_hbm.3) | copy-start | bytes 24580
where the time goes:
time: 50.8 us; the launch traced here: 50.4 us
  Pallas kernels  42.3 us (83%)
  local copies, waits for them, and re-layouts  7.4 us (15%)
  between operations  0.68 us (1%)
    pallas_call x1, Pallas kernels, exchange(): pl.pallas_call(functools.partial(exchange_kernel, n_gy, n_gx), out_shape=...  27.5 us
    pallas_call x1, Pallas kernels, columns(): pl.pallas_call(functools.partial(column_kernel, n_gy), out_shape=(jax.Sha...  14.8 us
    unnamed x20, local copies, waits for them, and re-layouts  7.4 us

commit v1 on v0

--- a/solution.py
+++ b/solution.py
@@ -20,7 +20,7 @@
 ECOLOGY = 0.2
 
 MESH = pl.DeviceIdType.MESH
-ANY = pl.BlockSpec(memory_space=pl.ANY)
+HBM = pl.BlockSpec(memory_space=pltpu.HBM)
 
 T = 30
 Z = 24
@@ -440,8 +440,8 @@
     return pl.pallas_call(
         functools.partial(exchange_kernel, n_gy, n_gx),
         out_shape=out_shape,
-        in_specs=[ANY] * 7,
-        out_specs=(ANY,) * 9,
+        in_specs=[HBM] * 7,
+        out_specs=(HBM,) * 9,
         scratch_shapes=[
             pltpu.VMEM((PLANES, FOLDED + 16, X), f32),
             pltpu.VMEM((T * Z * Y, X), f32),
@@ -474,7 +474,7 @@
             dma((3,)),
         ],
         compiler_params=pltpu.CompilerParams(
-            collective_id=0, has_side_effects=True, vmem_limit_bytes=32 * 1024 * 1024
+            collective_id=0, has_side_effects=True, vmem_limit_bytes=60 * 1024 * 1024
         ),
         name="exchange",
     )(u, v, eta, conc, land, bottom, coupling)
@@ -758,8 +758,8 @@
             jax.ShapeDtypeStruct((T, Z, Y, X), f32),
             jax.ShapeDtypeStruct((FOLDED, X), f32),
         ),
-        in_specs=[ANY] * 13,
-        out_specs=(ANY, ANY),
+        in_specs=[HBM] * 13,
+        out_specs=(HBM, HBM),
         scratch_shapes=[
             pltpu.VMEM((T, Z, 32, X), f32),
             pltpu.VMEM((T, Z + 1, Y, X), f32),
@@ -787,7 +787,7 @@
             dma((Z // Z_PART,)),
             dma((T // T_PART + 1,)),
         ],
-        compiler_params=pltpu.CompilerParams(vmem_limit_bytes=48 * 1024 * 1024),
+        compiler_params=pltpu.CompilerParams(vmem_limit_bytes=60 * 1024 * 1024),
         name="columns",
     )(conc, *parts, eta, land, bottom)
 

time: 50.8 us -> 42.6 us (0.84)
  local copies, waits for them, and re-layouts: 7.4 us -> 0 us
    unnamed x20 -> x0, local copies, waits for them, and re-layouts: 7.4 us -> none
    pallas_call x1, Pallas kernels: 27.5 us -> 26.7 us  [exchange(): pl.pallas_call(functools.partial(exchange_kernel, n_gy, n_gx), out_shape=...]
where the time goes in v1:
time: 42.6 us; the launch traced here: 42.4 us
  Pallas kernels  41.8 us (98%)
  between operations  0.64 us (2%)
    pallas_call x1, Pallas kernels, exchange(): pl.pallas_call(functools.partial(exchange_kernel, n_gy, n_gx), out_shape=...  26.7 us
    pallas_call x1, Pallas kernels, columns(): pl.pallas_call(functools.partial(column_kernel, n_gy), out_shape=(jax.Sha...  15.1 us

profile of v1, /device:TPU:1, one launch (start us, length us, event | category | flops | bytes accessed | tf_op | source)
XLA Modules:
  0.0 42.4 jit_solution(4675119131740230802)
XLA Ops:
  0.6 26.7 %exchange.1 = (f32[4,256,128]{2,1,0:T(8,128)}, f32[728,128]{1,0:T(8,128)}, f32[728,128]{1,0:T(8,128)}, f32[200,128]{1,0:T(8,128)}, f32[200,128]{1,0:T(8,128)}, /...) custom-call(f32[6,64,128]{2,1,0:T(8,128)} %bitcast.6, ...), custom_call_target="tpu_custom_call" | custom-call | tf_op jit(solution)/shard_map/exchange/pallas_call | solution.py:440
  27.3 15.1 %columns.1 = (f32[30,24,16,128]{3,2,1,0:T(8,128)}, f32[64,128]{1,0:T(8,128)}) custom-call(f32[30,24,16,128]{3,2,1,0:T(8,128)} %c_hbm.1, f32[4,256,128]{2,1,0:T(8,128)} %get-tuple-element.13.tiles_hbm, f32[728,128]{1,0:T(8,128)} %get-tuple-element.14.south_rows_hbm, f32[728,128]{1,0:T(8,128)} %get-tuple-element.15.north_rows_hbm, ...), custom_call_target="tpu_custom_call" | custom-call | tf_op jit(solution)/shard_map/columns/pallas_call | solution.py:755

commit v2 on v1

v2 whole, which is shorter than its diff:
```python
import functools

import jax
import jax.numpy as jnp
from jax import lax
from jax.experimental import pallas as pl
from jax.experimental.pallas import tpu as pltpu
from jax.sharding import PartitionSpec as P

CORIOLIS = 0.5
GRAVITY = 0.3
VISCOSITY = 0.1
TIME_STEP = 0.2
BAROTROPIC = 0.5
ADVECTION = 0.15
MIXING = 0.5
KAPPA_BASE = 0.1
KAPPA_SHEAR = 2.0
SHEAR_SCALE = 1.0
ECOLOGY = 0.2

MESH = pl.DeviceIdType.MESH
HBM = pl.BlockSpec(memory_space=pltpu.HBM)

T = 30
Z = 24
G = 4
L = Z // G
Y = 16
X = 128
PLANES = 2 * L + 1
FOLDED = Y * G
TILE_ROWS = 2 * L * Y
EDGE_ROWS = T * Z + 8
EDGE_COLS = Z // 2 * 8 + 8


def roll(x, by, axis):
    by = by % x.shape[axis]
    return x if by == 0 else pltpu.roll(x, by, axis)


def lanes(shape):
    return lax.broadcasted_iota(jnp.int32, shape, len(shape) - 1)


def rows(shape):
    return lax.broadcasted_iota(jnp.int32, shape, 0)


def exchange_kernel(
    n_gy,
    n_gx,
    u_hbm,
    v_hbm,
    eta_hbm,
    c_hbm,
    land_hbm,
    bottom_hbm,
    coupling_hbm,
    flow_u_out,
    flow_v_out,
    west_u_out,
    south_v_out,
    south_rows,
    north_rows,
    west_cols,
    east_cols,
    mix_hi_out,
    mix_lo_out,
    surface_out,
    planes,
    conc,
    land,
    bottom,
    coupling,
    edge_q,
    west_q,
    east_q,
    send_tile,
    send_up,
    send_down,
    send_col,
    tiles,
    from_south,
    from_north,
    from_west,
    from_east,
    from_sw,
    from_nw,
    from_se,
    spread_sum,
    spreads,
    push,
    flow_u,
    flow_v,
    west_u,
    south_v,
    row_lo,
    row_hi,
    col_east,
    col_west,
    mix_hi,
    mix_lo,
    surface,
    load_sem,
    conc_sem,
    send_sem,
    recv_sem,
    group_send,
    group_recv,
    store_sem,
):
    g = lax.axis_index("group")
    j = lax.axis_index("gy")
    i = lax.axis_index("gx")
    i_east = lax.rem(i + 1, n_gx)
    i_west = lax.rem(i + n_gx - 1, n_gx)
    has_south = j > 0
    has_north = j < n_gy - 1
    up = lax.div(i + 1, n_gx)
    down = (1 - lax.div(i + n_gx - 1, n_gx)) * (G - 1)

    loads = [
        pltpu.make_async_copy(u_hbm, planes.at[pl.ds(0, L), pl.ds(8, FOLDED)], load_sem.at[0]),
        pltpu.make_async_copy(v_hbm, planes.at[pl.ds(L, L), pl.ds(8, FOLDED)], load_sem.at[1]),
        pltpu.make_async_copy(eta_hbm, planes.at[2 * L, pl.ds(8, FOLDED)], load_sem.at[2]),
        pltpu.make_async_copy(land_hbm, land, load_sem.at[3]),
        pltpu.make_async_copy(bottom_hbm, bottom, load_sem.at[4]),
        pltpu.make_async_copy(coupling_hbm, coupling, load_sem.at[5]),
    ]
    for load in loads:
        load.start()
    conc_load = pltpu.make_async_copy(c_hbm, conc, conc_sem.at[0])
    conc_load.start()

    barrier = pltpu.get_barrier_semaphore()

    def greet(*device):
        pl.semaphore_signal(barrier, inc=1, device_id=device, device_id_type=MESH)

    for d in range(G):
        greet(d, j, i_east)
        greet(d, j, i_west)

    @pl.when(has_south)
    def _():
        for d in range(G):
            greet(d, j - 1, i_west)
            greet(d, j - 1, i_east)
            greet(d, j - 1, i)

    @pl.when(has_north)
    def _():
        for d in range(G):
            greet(d, j + 1, i_west)
            greet(d, j + 1, i)

    for d in range(1, G):
        greet(lax.rem(g + d, G), j, i)

    for load in loads:
        load.wait()
    lane = lanes((FOLDED, X))
    packed = jnp.zeros((FOLDED, X), jnp.float32)
    for p in range(PLANES):
        packed = jnp.where(lane // 4 == p, roll(planes[p, 8 : 8 + FOLDED, :], 4 * p + 2, 1), packed)
    edge_q[...] = packed
    flat = planes.reshape(PLANES * (FOLDED + 16), X)
    step = FOLDED + 16
    v_at = L * step
    top = 8 + (Y - 1) * G
    for f in range(G):
        send_col[f] = edge_q[pl.ds(f, Y, stride=G), :]
        send_up[f] = jnp.zeros((24, X), jnp.float32)
        send_up[f, pl.ds(0, L), :] = flat[pl.ds(top + f, L, stride=step), :]
        send_up[f, pl.ds(L, L), :] = flat[pl.ds(v_at + top + f, L, stride=step), :]
        send_up[f, pl.ds(2 * L, L), :] = flat[pl.ds(v_at + top - G + f, L, stride=step), :]
        send_down[f] = jnp.zeros((16, X), jnp.float32)
        send_down[f, pl.ds(0, L), :] = flat[pl.ds(8 + f, L, stride=step), :]
        send_down[f, pl.ds(L, L), :] = flat[pl.ds(v_at + 8 + f, L, stride=step), :]
        for p in range(2 * L):
            send_tile[f, pl.ds(p * Y, Y), :] = flat[pl.ds(p * step + 8 + f, Y, stride=G), :]

    south_count = lax.div(j + n_gy - 1, n_gy)
    north_count = lax.div(2 * (n_gy - 1) - j, n_gy)
    pl.semaphore_wait(barrier, G - 1 + 2 * G + 2 * G * south_count + 3 * G * north_count)

    def remote(src, dst, n, device):
        return pltpu.make_async_remote_copy(
            src_ref=src,
            dst_ref=dst,
            send_sem=send_sem.at[n],
            recv_sem=recv_sem.at[n],
            device_id=device,
            device_id_type=MESH,
        )

    def spread_out(kind, src, dst, f, m, device):
        return pltpu.make_async_remote_copy(
            src_ref=src,
            dst_ref=dst.at[m],
            send_sem=group_send.at[kind, f],
            recv_sem=group_recv.at[kind, m],
            device_id=device,
            device_id_type=MESH,
        )

    def corner_ne(f, m):
        device = (lax.rem(f + up, G), j + 1, i_east)
        return spread_out(0, send_col.at[f, pl.ds(8, 8)], from_sw, f, m, device)

    def corner_se(f, m):
        device = (lax.rem(f + up, G), j - 1, i_east)
        return spread_out(1, send_col.at[f, pl.ds(0, 8)], from_nw, f, m, device)

    def corner_nw(f, m):
        device = (lax.rem(f + down, G), j + 1, i_west)
        return spread_out(2, send_col.at[f, pl.ds(8, 8)], from_se, f, m, device)

    def col_to_east(f, m):
        return spread_out(
            3, send_col.at[f], from_west, f, m, (lax.rem(f + up, G), j, i_east)
        )

    def col_to_west(f, m):
        return spread_out(
            4, send_col.at[f], from_east, f, m, (lax.rem(f + down, G), j, i_west)
        )

    def row_to_north(f, m):
        return spread_out(5, send_up.at[f], from_south, f, m, (f, j + 1, i))

    def row_to_south(f, m):
        return spread_out(6, send_down.at[f], from_north, f, m, (f, j - 1, i))

    def tile_to(f, m):
        return spread_out(7, send_tile.at[f], tiles, f, m, (f, j, i))

    def part_to(f, m):
        return spread_out(8, spread_sum, spreads, f, m, (f, j, i))

    to_north = remote(
        planes.at[pl.ds(L, L + 1), pl.ds(FOLDED, 8)],
        planes.at[pl.ds(L, L + 1), pl.ds(0, 8)],
        0,
        (g, j + 1, i),
    )
    to_south = remote(
        planes.at[2 * L, pl.ds(8, 8)], planes.at[2 * L, pl.ds(8 + FOLDED, 8)], 1, (g, j - 1, i)
    )
    to_east = remote(edge_q, west_q, 2, (g, j, i_east))
    to_west = remote(edge_q, east_q, 3, (g, j, i_west))
    rows_north = remote(row_hi, south_rows, 4, (g, j + 1, i))
    rows_south = remote(row_lo, north_rows, 5, (g, j - 1, i))
    cols_east = remote(col_east, west_cols, 6, (lax.rem(g + up, G), j, i_east))
    cols_west = remote(col_west, east_cols, 7, (lax.rem(g + down, G), j, i_west))

    @pl.when(has_north)
    def _():
        for f in range(G):
            corner_ne(f, g).start()
            corner_nw(f, g).start()

    @pl.when(has_south)
    def _():
        for f in range(G):
            corner_se(f, g).start()

    for f in range(G):
        col_to_east(f, g).start()
        col_to_west(f, g).start()
    to_east.start()
    to_west.start()
    for d in (2, 1, 3):
        tile_to(lax.rem(g + d, G), g).start()

    @pl.when(has_north)
    def _():
        to_north.start()
        for f in range(G):
            row_to_north(f, g).start()

    @pl.when(has_south)
    def _():
        to_south.start()
        for f in range(G):
            row_to_south(f, g).start()

    tiles[g] = send_tile[g]

    depth = jnp.where(land[...] > 0, bottom[...], 0).astype(jnp.float32)
    conc_load.wait()
    small = lanes((8, X))

    def take_cols(pair, carry):
        to_e = [jnp.zeros((8, X), jnp.float32) for _ in range(4)]
        to_w = [jnp.zeros((8, X), jnp.float32) for _ in range(4)]
        for half in range(2):
            for t in range(T):
                for o in range(2):
                    base = pl.multiple_of((t * Z + 2 * pair + half) * Y + 8 * o, 8)
                    spot = 64 * o + 2 * t + half
                    turned = roll(conc[pl.ds(base, 8), :], spot + 1, 1)
                    n = (2 * t + o) % 4
                    to_e[n] = jnp.where(small == spot, turned, to_e[n])
                    to_w[n] = jnp.where(small == spot + 1, turned, to_w[n])
        place = pl.ds(pl.multiple_of(pair * 8, 8), 8)
        col_east[place, :] = (to_e[0] + to_e[1]) + (to_e[2] + to_e[3])
        col_west[place, :] = roll((to_w[0] + to_w[1]) + (to_w[2] + to_w[3]), -1, 1)
        return carry

    lax.fori_loop(0, Z // 2, take_cols, 0)
    last = pl.ds(Z // 2 * 8, 8)
    col_east[last, :] = jnp.where(small < 64, roll(depth[0:8], 1, 1), roll(depth[8:16], 65, 1))
    col_west[last, :] = jnp.where(small < 64, depth[0:8], roll(depth[8:16], 64, 1))
    cols_east.start()
    cols_west.start()

    row_lo[pl.ds(T * Z, 8), :] = jnp.broadcast_to(depth[0:1], (8, X))
    row_hi[pl.ds(T * Z, 8), :] = jnp.broadcast_to(depth[Y - 1 : Y], (8, X))

    def take_rows(t, carry):
        base = pl.multiple_of(t * (Z * Y), Z * Y)
        place = pl.multiple_of(t * Z, 8)
        row_lo[pl.ds(place, Z), :] = conc[pl.ds(base, Z, stride=Y), :]
        row_hi[pl.ds(place, Z), :] = conc[pl.ds(base + Y - 1, Z, stride=Y), :]
        return carry

    lax.fori_loop(0, T, take_rows, 0)

    @pl.when(has_north)
    def _():
        rows_north.start()

    @pl.when(has_south)
    def _():
        rows_south.start()

    tall = (rows((8 * T, T)) // 8 == lanes((8 * T, T))).astype(jnp.bfloat16)
    wide = (rows((T, 8 * T)) == lanes((T, 8 * T)) // 8).astype(jnp.bfloat16)
    own = lax.rem(rows((8 * T, 8 * T)), 8) == lax.rem(lanes((8 * T, 8 * T)), 8)
    hi = coupling[...].astype(jnp.bfloat16)
    lo = (coupling[...] - hi.astype(jnp.float32)).astype(jnp.bfloat16)
    for part, place in ((hi, mix_hi), (lo, mix_lo)):
        half = jnp.dot(tall, part, preferred_element_type=jnp.float32).astype(jnp.bfloat16)
        whole = jnp.dot(half, wide, preferred_element_type=jnp.float32)
        place[...] = jnp.where(own, whole, 0.0).astype(jnp.bfloat16)
    stores = [
        pltpu.make_async_copy(mix_hi, mix_hi_out, store_sem.at[0]),
        pltpu.make_async_copy(mix_lo, mix_lo_out, store_sem.at[1]),
    ]
    for store in stores:
        store.start()

    @pl.when(has_south)
    def _():
        to_north.wait_recv()

    @pl.when(has_north)
    def _():
        to_south.wait_recv()

    @pl.when(jnp.logical_not(has_south))
    def _():
        planes[pl.ds(L, L + 1), pl.ds(0, 8), :] = jnp.zeros((L + 1, 8, X), jnp.float32)

    @pl.when(jnp.logical_not(has_north))
    def _():
        planes[2 * L, pl.ds(8 + FOLDED, 8), :] = jnp.zeros((8, X), jnp.float32)

    to_east.wait_recv()
    to_west.wait_recv()
    fold = lax.rem(rows((FOLDED, X)), G)
    qw = west_q[...]
    qe = east_q[...]
    qw_turned = jnp.where(fold == 0, roll(qw, -(G - 1), 0), roll(qw, 1, 0))
    qe_turned = jnp.where(fold == G - 1, roll(qe, G - 1, 0), roll(qe, -1, 0))
    qw = jnp.where(i == 0, qw_turned, qw)
    qe = jnp.where(i == n_gx - 1, qe_turned, qe)
    spread = jnp.zeros((FOLDED, X), jnp.float32)
    for k in range(L):
        u = planes[k, 8 : 8 + FOLDED, :]
        v = planes[L + k, 8 : 8 + FOLDED, :]
        u_west = jnp.where(lane == 0, roll(qw, -(4 * k + 1), 1), roll(u, 1, 1))
        spread = spread + (u - u_west + v - planes[L + k, 8 - G : 8 - G + FOLDED, :])
    spread_sum[...] = spread
    for d in (2, 1, 3):
        part_to(lax.rem(g + d, G), g).start()
    spreads[g] = spread

    e = 4 * (2 * L)
    height = planes[2 * L, 8 : 8 + FOLDED, :]
    height_east = jnp.where(lane == X - 1, roll(qe, X - 1 - (e + 2), 1), roll(height, -1, 1))
    push[0:FOLDED, :] = GRAVITY * (height_east - height)
    push[FOLDED : 2 * FOLDED, :] = GRAVITY * (height - roll(qw, -(e + 1), 1))
    push[2 * FOLDED : 3 * FOLDED, :] = GRAVITY * (
        planes[2 * L, 8 + G : 8 + G + FOLDED, :] - height
    )
    push[3 * FOLDED : 3 * FOLDED + 8, :] = GRAVITY * (
        planes[2 * L, 8:16, :] - planes[2 * L, 8 - G : 16 - G, :]
    )
    push_east = push[pl.ds(g, Y, stride=G), :]
    push_west = push[pl.ds(FOLDED + g, Y, stride=G), :]
    push_west = jnp.broadcast_to(push_west[:, 0:1], (Y, X))
    push_north = push[pl.ds(2 * FOLDED + g, Y, stride=G), :]
    push_south = jnp.broadcast_to(push[pl.ds(3 * FOLDED + g, 1), :], (8, X))

    for d in range(1, G):
        tile_to(lax.rem(g + d, G), lax.rem(g + d, G)).wait_recv()
    for m in range(G):
        col_to_east(m, m).wait_recv()
        col_to_west(m, m).wait_recv()

    @pl.when(has_south)
    def _():
        for m in range(G):
            corner_ne(m, m).wait_recv()
            corner_nw(m, m).wait_recv()
            row_to_north(m, m).wait_recv()

    @pl.when(has_north)
    def _():
        for m in range(G):
            corner_se(m, m).wait_recv()
            row_to_south(m, m).wait_recv()

    line = lanes((Y, X))
    deep = rows((Y, X))

    def over(row, shape=(Y, X)):
        return jnp.broadcast_to(row, shape)

    for m in range(G):
        south = jnp.where(has_south, from_south[m], 0.0)
        north = jnp.where(has_north, from_north[m], 0.0)
        sw = jnp.where(has_south, from_sw[m], 0.0)[7:8]
        se = jnp.where(has_south, from_se[m], 0.0)[7:8]
        nw = jnp.where(has_north, from_nw[m], 0.0)[0:1]
        west = from_west[m]
        side = jnp.where(line % 4 == 1, west, roll(from_east[m], -2, 1))
        first = jnp.zeros((Y, X), jnp.float32)
        below = jnp.zeros((8, X), jnp.float32)
        sw8 = over(sw, (8, X))
        se8 = over(se, (8, X))
        for k in range(L):
            u = tiles[m, pl.ds(k * Y, Y), :]
            v = tiles[m, pl.ds((L + k) * Y, Y), :]

            def laplacian(x, p):
                edge = roll(side, -(4 * p + 1), 1)
                return (
                    jnp.where(line == X - 1, edge, roll(x, -1, 1))
                    + jnp.where(line == 0, edge, roll(x, 1, 1))
                    + jnp.where(deep == Y - 1, over(north[p : p + 1]), roll(x, -1, 0))
                    + jnp.where(deep == 0, over(south[p : p + 1]), roll(x, 1, 0))
                    - 4.0 * x
                )

            flow_u[m * L + k] = u + TIME_STEP * (
                CORIOLIS * v - push_east + VISCOSITY * laplacian(u, k)
            )
            flow_v[m * L + k] = v + TIME_STEP * (
                -CORIOLIS * u - push_north + VISCOSITY * laplacian(v, L + k)
            )
            spot = 4 * k + 1
            first = jnp.where(line == spot, roll(u, spot, 1), first)
            p = L + k
            a = over(south[p : p + 1], (8, X))
            lap = (
                jnp.where(small == X - 1, roll(se8, X - 1 - (4 * p + 2), 1), roll(a, -1, 1))
                + jnp.where(small == 0, roll(sw8, -(4 * p + 1), 1), roll(a, 1, 1))
                + over(v[0:1], (8, X))
                + over(south[2 * L + k : 2 * L + k + 1], (8, X))
                - 4.0 * a
            )
            a = a + TIME_STEP * (
                -CORIOLIS * over(south[k : k + 1], (8, X)) - push_south + VISCOSITY * lap
            )
            below = jnp.where(rows((8, X)) == k, a, below)
        south_v[m] = below
        west_north = jnp.where(deep == Y - 1, over(nw), roll(west, -1, 0))
        west_south = jnp.where(deep == 0, over(sw), roll(west, 1, 0))
        lap = first + roll(west, 1, 1) + west_north + west_south - 4.0 * west
        west_u[m] = west + TIME_STEP * (
            CORIOLIS * roll(west, -4 * L, 1) - push_west + VISCOSITY * lap
        )
    flows = [
        pltpu.make_async_copy(flow_u, flow_u_out, store_sem.at[2]),
        pltpu.make_async_copy(flow_v, flow_v_out, store_sem.at[3]),
        pltpu.make_async_copy(west_u, west_u_out, store_sem.at[4]),
        pltpu.make_async_copy(south_v, south_v_out, store_sem.at[5]),
    ]
    for store in flows:
        store.start()

    for d in range(1, G):
        part_to(lax.rem(g + d, G), lax.rem(g + d, G)).wait_recv()
    surface[...] = planes[2 * L, 8 : 8 + FOLDED, :] - (BAROTROPIC / Z) * (
        (spreads[0] + spreads[1]) + (spreads[2] + spreads[3])
    )
    surface_store = pltpu.make_async_copy(surface, surface_out, store_sem.at[6])
    surface_store.start()

    for d in range(1, G):
        tile_to(lax.rem(g + d, G), g).wait_send()
        part_to(lax.rem(g + d, G), g).wait_send()
    for f in range(G):
        col_to_east(f, g).wait_send()
        col_to_west(f, g).wait_send()

    @pl.when(has_north)
    def _():
        to_north.wait_send()
        rows_north.wait_send()
        rows_south.wait_recv()
        for f in range(G):
            row_to_north(f, g).wait_send()
            corner_ne(f, g).wait_send()
            corner_nw(f, g).wait_send()

    @pl.when(has_south)
    def _():
        to_south.wait_send()
        rows_south.wait_send()
        rows_north.wait_recv()
        for f in range(G):
            row_to_south(f, g).wait_send()
            corner_se(f, g).wait_send()

    to_east.wait_send()
    to_west.wait_send()
    cols_east.wait()
    cols_west.wait()
    for store in stores + flows:
        store.wait()
    surface_store.wait()


def exchange(n_gy, n_gx, u, v, eta, conc, land, bottom, coupling):
    f32 = jnp.float32
    dma = pltpu.SemaphoreType.DMA
    mix = ((8 * T, 8 * T), jnp.bfloat16)
    out_shape = tuple(
        jax.ShapeDtypeStruct(*shape)
        for shape in (
            ((Z, Y, X), f32),
            ((Z, Y, X), f32),
            ((G, Y, X), f32),
            ((G, 8, X), f32),
            ((EDGE_ROWS, X), f32),
            ((EDGE_ROWS, X), f32),
            ((EDGE_COLS, X), f32),
            ((EDGE_COLS, X), f32),
            mix,
            mix,
            ((FOLDED, X), f32),
        )
    )
    return pl.pallas_call(
        functools.partial(exchange_kernel, n_gy, n_gx),
        out_shape=out_shape,
        in_specs=[HBM] * 7,
        out_specs=(HBM,) * len(out_shape),
        scratch_shapes=[
            pltpu.VMEM((PLANES, FOLDED + 16, X), f32),
            pltpu.VMEM((T * Z * Y, X), f32),
            pltpu.VMEM((Y, X), jnp.int32),
            pltpu.VMEM((Y, X), jnp.int32),
            pltpu.VMEM((T, T), f32),
            pltpu.VMEM((FOLDED, X), f32),
            pltpu.VMEM((FOLDED, X), f32),
            pltpu.VMEM((FOLDED, X), f32),
            pltpu.VMEM((G, TILE_ROWS, X), f32),
            pltpu.VMEM((G, 24, X), f32),
            pltpu.VMEM((G, 16, X), f32),
            pltpu.VMEM((G, Y, X), f32),
            pltpu.VMEM((G, TILE_ROWS, X), f32),
            pltpu.VMEM((G, 24, X), f32),
            pltpu.VMEM((G, 16, X), f32),
            pltpu.VMEM((G, Y, X), f32),
            pltpu.VMEM((G, Y, X), f32),
            pltpu.VMEM((G, 8, X), f32),
            pltpu.VMEM((G, 8, X), f32),
            pltpu.VMEM((G, 8, X), f32),
            pltpu.VMEM((FOLDED, X), f32),
            pltpu.VMEM((G, FOLDED, X), f32),
            pltpu.VMEM((3 * FOLDED + 8, X), f32),
            pltpu.VMEM((Z, Y, X), f32),
            pltpu.VMEM((Z, Y, X), f32),
            pltpu.VMEM((G, Y, X), f32),
            pltpu.VMEM((G, 8, X), f32),
            pltpu.VMEM((EDGE_ROWS, X), f32),
            pltpu.VMEM((EDGE_ROWS, X), f32),
            pltpu.VMEM((EDGE_COLS, X), f32),
            pltpu.VMEM((EDGE_COLS, X), f32),
            pltpu.VMEM(*mix),
            pltpu.VMEM(*mix),
            pltpu.VMEM((FOLDED, X), f32),
            dma((6,)),
            dma((1,)),
            dma((8,)),
            dma((8,)),
            dma((9, G)),
            dma((9, G)),
            dma((7,)),
        ],
        compiler_params=pltpu.CompilerParams(
            collective_id=0, has_side_effects=True, vmem_limit_bytes=60 * 1024 * 1024
        ),
        name="exchange",
    )(u, v, eta, conc, land, bottom, coupling)


Z_PART = 4
T_PART = 5
COEF = 9


def column_kernel(
    n_gy,
    c_hbm,
    flow_u_hbm,
    flow_v_hbm,
    west_u_hbm,
    south_v_hbm,
    south_rows_hbm,
    north_rows_hbm,
    west_cols_hbm,
    east_cols_hbm,
    mix_hi_hbm,
    mix_lo_hbm,
    surface_in,
    land_hbm,
    bottom_hbm,
    out_hbm,
    surface_hbm,
    conc,
    solved,
    coef,
    flow_u,
    flow_v,
    south_rows,
    north_rows,
    west_cols,
    east_cols,
    sides,
    west_u,
    south_v,
    mix_hi,
    mix_lo,
    land,
    bottom,
    adv_a,
    adv_b,
    hi_a,
    lo_a,
    hi_b,
    lo_b,
    load_sem,
    conc_sem,
    out_sem,
):
    j = lax.axis_index("gy")
    pairs = (
        (land_hbm, land),
        (bottom_hbm, bottom),
        (flow_u_hbm, flow_u),
        (flow_v_hbm, flow_v),
        (west_u_hbm, west_u),
        (south_v_hbm, south_v),
        (west_cols_hbm, west_cols),
        (east_cols_hbm, east_cols),
        (south_rows_hbm, south_rows),
        (north_rows_hbm, north_rows),
        (mix_hi_hbm, mix_hi),
        (mix_lo_hbm, mix_lo),
    )
    loads = [pltpu.make_async_copy(a, b, load_sem.at[n]) for n, (a, b) in enumerate(pairs)]
    for load in loads:
        load.start()
    conc_loads = [
        pltpu.make_async_copy(
            c_hbm.at[:, pl.ds(n * Z_PART, Z_PART)],
            conc.at[:, pl.ds(n * Z_PART, Z_PART), pl.ds(8, Y)],
            conc_sem.at[n],
        )
        for n in range(Z // Z_PART)
    ]
    for load in conc_loads:
        load.start()
    for load in loads:
        load.wait()

    flat = conc.reshape(T * Z * 32, X)
    south_ok = j > 0
    north_ok = j < n_gy - 1

    def put_rows(t, carry):
        place = pl.multiple_of(t * Z, 8)
        base = pl.multiple_of(t * (Z * 32), 8)
        flat[pl.ds(base + 7, Z, stride=32), :] = jnp.where(
            south_ok, south_rows[pl.ds(place, Z), :], 0.0
        )
        flat[pl.ds(base + 8 + Y, Z, stride=32), :] = jnp.where(
            north_ok, north_rows[pl.ds(place, Z), :], 0.0
        )
        return carry

    lax.fori_loop(0, T, put_rows, 0)

    lane = lanes((8, X))
    odd = lane % 2 == 1

    def put_cols(pair, carry):
        place = pl.ds(pl.multiple_of(pair * 8, 8), 8)
        west = west_cols[place, :]
        east = east_cols[place, :]
        first = pl.multiple_of(pair * 16, 8)
        sides[pl.ds(first, 8), :] = jnp.where(odd, roll(west, 1, 1), east)
        sides[pl.ds(first + 8, 8), :] = jnp.where(odd, west, roll(east, -1, 1))
        return carry

    lax.fori_loop(0, Z // 2 + 1, put_cols, 0)

    surface_store = pltpu.make_async_copy(surface_in, surface_hbm, out_sem.at[T // T_PART])
    surface_store.start()

    wide = lanes((Y, X))
    tall = rows((Y, X))
    depth = jnp.where(land[...] > 0, bottom[...], 0).astype(jnp.float32)
    depth_side = sides[pl.ds(Z * 8, 8), :]
    depth_side = jnp.concatenate([roll(depth_side, -1, 1), roll(depth_side, -65, 1)], axis=0)
    depth_east = jnp.where(wide == X - 1, depth_side, roll(depth, -1, 1))
    depth_west = jnp.where(wide == 0, depth_side, roll(depth, 1, 1))
    above = jnp.where(north_ok, north_rows[pl.ds(T * Z, 8), :], 0.0)
    below = jnp.where(south_ok, south_rows[pl.ds(T * Z, 8), :], 0.0)
    depth_north = jnp.where(
        tall == Y - 1, jnp.concatenate([above, above], axis=0), roll(depth, -1, 0)
    )
    depth_south = jnp.where(tall == 0, jnp.concatenate([below, below], axis=0), roll(depth, 1, 0))
    reach_east = jnp.minimum(depth, depth_east)
    reach_west = jnp.minimum(depth, depth_west)
    reach_north = jnp.minimum(depth, depth_north)
    reach_south = jnp.minimum(depth, depth_south)

    def flows(z):
        return flow_u[z], flow_v[z]

    g_above = jnp.zeros((Y, X), jnp.float32)
    r_above = jnp.zeros((Y, X), jnp.float32)
    u, v = flows(0)
    for z in range(Z):
        m, k = z // L, z % L
        u_west = jnp.where(wide == 0, roll(west_u[m], -(4 * k + 1), 1), roll(u, 1, 1))
        row = jnp.where(south_ok, south_v[m, k : k + 1, :], 0.0)
        v_south = jnp.where(tall == 0, jnp.broadcast_to(row, (Y, X)), roll(v, 1, 0))
        ke = jnp.where(reach_east > z, ADVECTION, 0.0)
        kw = jnp.where(reach_west > z, ADVECTION, 0.0)
        kn = jnp.where(reach_north > z, ADVECTION, 0.0)
        ks = jnp.where(reach_south > z, ADVECTION, 0.0)
        coef[z, 0] = (
            1.0
            - ke * jnp.maximum(u, 0.0)
            + kw * jnp.minimum(u_west, 0.0)
            - kn * jnp.maximum(v, 0.0)
            + ks * jnp.minimum(v_south, 0.0)
        )
        coef[z, 1] = -ke * jnp.minimum(u, 0.0)
        coef[z, 2] = kw * jnp.maximum(u_west, 0.0)
        coef[z, 3] = -kn * jnp.minimum(v, 0.0)
        coef[z, 4] = ks * jnp.maximum(v_south, 0.0)
        if z < Z - 1:
            u_next, v_next = flows(z + 1)
            shear = (u - u_next) ** 2 + (v - v_next) ** 2
            rate = KAPPA_BASE + KAPPA_SHEAR * shear / (shear + SHEAR_SCALE)
            g = jnp.where(depth > z + 1, MIXING * rate, 0.0)
            u, v = u_next, v_next
        else:
            g = jnp.zeros((Y, X), jnp.float32)
        inverse = 1.0 / (1.0 + g_above + g - g_above * r_above)
        coef[z, 5] = inverse
        coef[z, 6] = jnp.where(depth > z, ECOLOGY * inverse, 0.0)
        coef[z, 7] = g_above * inverse
        r_above = g * inverse
        coef[z, 8] = r_above
        g_above = g

    def zero_top(t, carry):
        solved[t, 0] = jnp.zeros((Y, X), jnp.float32)
        return carry

    lax.fori_loop(0, T, zero_top, 0)

    def advance(z, adv, hi_ref, lo_ref):
        side = sides[pl.ds(pl.multiple_of(z * 8, 8), 8), :]
        for o in range(2):
            ks = [coef[z, n, 8 * o : 8 * o + 8, :] for n in range(5)]
            for pair in range(T // 2):
                both = []
                for t in (2 * pair, 2 * pair + 1):
                    c = conc[t, z, 8 + 8 * o : 16 + 8 * o, :]
                    edge = roll(side, -(64 * o + 2 * t + 1), 1)
                    east = jnp.where(lane == X - 1, edge, roll(c, -1, 1))
                    west = jnp.where(lane == 0, edge, roll(c, 1, 1))
                    north = conc[t, z, 9 + 8 * o : 17 + 8 * o, :]
                    south = conc[t, z, 7 + 8 * o : 15 + 8 * o, :]
                    a = (ks[0] * c + ks[1] * east) + (
                        ks[2] * west + (ks[3] * north + ks[4] * south)
                    )
                    adv[t, 8 * o : 8 * o + 8, :] = a
                    both.append(jnp.tanh(a))
                y = jnp.concatenate(both, axis=0)
                hi = y.astype(jnp.bfloat16)
                lo = (y - hi.astype(jnp.float32)).astype(jnp.bfloat16)
                hi_ref[16 * pair : 16 * pair + 16, o * X : o * X + X] = hi
                lo_ref[16 * pair : 16 * pair + 16, o * X : o * X + X] = lo

    def mix(hi_ref, lo_ref):
        return (
            jnp.dot(mix_hi[...], hi_ref[...], preferred_element_type=jnp.float32)
            + jnp.dot(mix_lo[...], hi_ref[...], preferred_element_type=jnp.float32)
            + jnp.dot(mix_hi[...], lo_ref[...], preferred_element_type=jnp.float32)
        )

    def finish(z, adv, source):
        for o in range(2):
            ks = [coef[z, n, 8 * o : 8 * o + 8, :] for n in range(5, 8)]
            for t in range(T):
                s = source[8 * t : 8 * t + 8, o * X : o * X + X]
                solved[t, z + 1, 8 * o : 8 * o + 8, :] = (
                    ks[0] * adv[t, 8 * o : 8 * o + 8, :]
                    + ks[1] * s
                    + ks[2] * solved[t, z, 8 * o : 8 * o + 8, :]
                )

    def two(i, carry):
        z = 2 * i

        source = mix(hi_a, lo_a)
        advance(z + 1, adv_b, hi_b, lo_b)
        finish(z, adv_a, source)
        source = mix(hi_b, lo_b)
        advance(z + 2, adv_a, hi_a, lo_a)
        finish(z + 1, adv_b, source)
        return carry

    for load in conc_loads:
        load.wait()
    advance(0, adv_a, hi_a, lo_a)
    lax.fori_loop(0, Z // 2 - 1, two, 0)
    source = mix(hi_a, lo_a)
    advance(Z - 1, adv_b, hi_b, lo_b)
    finish(Z - 2, adv_a, source)
    finish(Z - 1, adv_b, mix(hi_b, lo_b))

    def store(n):
        return pltpu.make_async_copy(
            solved.at[pl.ds(n * T_PART, T_PART), pl.ds(1, Z)],
            out_hbm.at[pl.ds(n * T_PART, T_PART)],
            out_sem.at[n],
        )

    def back(n, carry):
        base = n * T_PART
        x = [solved[base + t, Z] for t in range(T_PART)]
        for z in range(Z - 2, -1, -1):
            r = coef[z, 8]
            for t in range(T_PART):
                x[t] = solved[base + t, z + 1] + r * x[t]
                solved[base + t, z + 1] = x[t]
        store(n).start()
        return carry

    lax.fori_loop(0, T // T_PART, back, 0)
    for n in range(T // T_PART):
        store(n).wait()
    surface_store.wait()


def columns(n_gy, conc, parts, land, bottom):
    f32 = jnp.float32
    dma = pltpu.SemaphoreType.DMA
    mix_type = pltpu.VMEM((8 * T, 2 * X), jnp.bfloat16)
    return pl.pallas_call(
        functools.partial(column_kernel, n_gy),
        out_shape=(
            jax.ShapeDtypeStruct((T, Z, Y, X), f32),
            jax.ShapeDtypeStruct((FOLDED, X), f32),
        ),
        in_specs=[HBM] * 14,
        out_specs=(HBM, HBM),
        scratch_shapes=[
            pltpu.VMEM((T, Z, 32, X), f32),
            pltpu.VMEM((T, Z + 1, Y, X), f32),
            pltpu.VMEM((Z, COEF, Y, X), f32),
            pltpu.VMEM((Z, Y, X), f32),
            pltpu.VMEM((Z, Y, X), f32),
            pltpu.VMEM((EDGE_ROWS, X), f32),
            pltpu.VMEM((EDGE_ROWS, X), f32),
            pltpu.VMEM((EDGE_COLS, X), f32),
            pltpu.VMEM((EDGE_COLS, X), f32),
            pltpu.VMEM((2 * EDGE_COLS, X), f32),
            pltpu.VMEM((G, Y, X), f32),
            pltpu.VMEM((G, 8, X), f32),
            pltpu.VMEM((8 * T, 8 * T), jnp.bfloat16),
            pltpu.VMEM((8 * T, 8 * T), jnp.bfloat16),
            pltpu.VMEM((Y, X), jnp.int32),
            pltpu.VMEM((Y, X), jnp.int32),
            pltpu.VMEM((T, Y, X), f32),
            pltpu.VMEM((T, Y, X), f32),
            mix_type,
            mix_type,
            mix_type,
            mix_type,
            dma((12,)),
            dma((Z // Z_PART,)),
            dma((T // T_PART + 1,)),
        ],
        compiler_params=pltpu.CompilerParams(vmem_limit_bytes=60 * 1024 * 1024),
        name="columns",
    )(conc, *parts, land, bottom)


def shards(east_velocity, north_velocity, sea_surface, tracers, land_sea, bottom_level, coupling):
    n_gy = lax.axis_size("gy")
    n_gx = lax.axis_size("gx")
    eta = sea_surface.reshape(FOLDED, X)
    parts = exchange(
        n_gy,
        n_gx,
        east_velocity.reshape(L, FOLDED, X),
        north_velocity.reshape(L, FOLDED, X),
        eta,
        tracers.reshape(T * Z * Y, X),
        land_sea,
        bottom_level,
        coupling,
    )
    tracers_next, surface_next = columns(n_gy, tracers, parts, land_sea, bottom_level)
    return tracers_next, surface_next.reshape(Y, G, X)


def solution(mesh):
    placed = (
        P("group", "gy", None, "gx"),
        P("group", "gy", None, "gx"),
        P("gy", None, "gx"),
        P(None, None, "gy", ("group", "gx")),
        P("gy", ("group", "gx")),
        P("gy", ("group", "gx")),
        P(),
    )
    return jax.shard_map(
        shards,
        mesh=mesh,
        in_specs=placed,
        out_specs=(P(None, None, "gy", ("group", "gx")), P("gy", None, "gx")),
        check_vma=False,
    )
```

time: 42.6 us -> 36.9 us (0.87)
  Pallas kernels: 41.8 us -> 36.1 us
    pallas_call x1, Pallas kernels: 26.7 us -> 21.9 us  [exchange(): pl.pallas_call(functools.partial(exchange_kernel, n_gy, n_gx), out_shape=...]
    pallas_call x1, Pallas kernels: 15.1 us -> 14.2 us  [columns(): pl.pallas_call(functools.partial(column_kernel, n_gy), out_shape=(jax.Sha...]
where the time goes in v2:
time: 36.9 us; the launch traced here: 36.7 us
  Pallas kernels  36.1 us (98%)
  between operations  0.64 us (2%)
    pallas_call x1, Pallas kernels, exchange(): pl.pallas_call(functools.partial(exchange_kernel, n_gy, n_gx), out_shape=...  21.9 us
    pallas_call x1, Pallas kernels, columns(): pl.pallas_call(functools.partial(column_kernel, n_gy), out_shape=(jax.Sha...  14.2 us

profile of v2, /device:TPU:1, one launch (start us, length us, event | category | flops | bytes accessed | tf_op | source)
XLA Modules:
  0.0 36.7 jit_solution(16057003377434802020)
XLA Ops:
  0.6 21.9 %exchange.1 = (f32[24,16,128]{2,1,0:T(8,128)}, f32[24,16,128]{2,1,0:T(8,128)}, f32[4,16,128]{2,1,0:T(8,128)}, f32[4,8,128]{2,1,0:T(8,128)}, f32[728,128]{1,0:T(8...) custom-call(f32[6,64,128]{2,1,0:T(8,128)} %bitcast.6, ...), custom_call_target="tpu_custom_call" | custom-call | tf_op jit(solution)/shard_map/exchange/pallas_call | solution.py:560
  22.5 14.2 %columns.1 = (f32[30,24,16,128]{3,2,1,0:T(8,128)}, f32[64,128]{1,0:T(8,128)}) custom-call(f32[30,24,16,128]{3,2,1,0:T(8,128)} %c_hbm.1, f32[24,16,128]{2,1,0:T(8,128)} %get-tuple-element.15.flow_u_hbm, f32[24,16,128]{2,1,0:T(8,128)} %get-tuple-element.16.flow_v_hbm, f32[4,16,128]{2,1,0:T(8,128)} %get-tuple-element.17.west_u_hbm, ...), custom_call_target="tpu_custom_call" | custom-call | tf_op jit(solution)/shard_map/columns/pallas_call | solution.py:885
